TPU v7x, 32 devices: a whole 2x2x4 slice. The times are simulated.
32 devices in a mesh: parts: 2 (over y), tm: 8 (over z, x), chan: 2 (over core).
Axes of the slice: x: 2, y: 2, z: 4, core: 2. Of those that a mesh axis runs over, the one named last changes fastest.
Arguments:
- signal: bfloat16 [16384, 1024], P(('parts', 'tm'), 'chan'), parts along dimension 0, may hold values from -6 to 6
- kernel_weight_stack: bfloat16 [2, 16, 128, 128], P(None, 'chan'), may hold values from -0.5 to 0.5
- conv_bias: float32 [2, 16, 128], P(None, 'chan'), may hold values from -4 to 4
- mix_weight: bfloat16 [2, 1024, 1024], P(None, None, 'chan'), may hold values from -0.1875 to 0.1875
Outputs:
- output: bfloat16 [16384, 1024], P(('parts', 'tm'), 'chan'), parts along dimension 0
There are 2 independent parts, one for each index of `parts`. A program takes and returns all parts, laid end to end along the dimension named above; an argument that names none is the same for every part. Nothing has to cross between parts.
All inputs are finite; a program needn't handle non-finite values.
Results may differ from a plain program's by a relative error of at most 0.0049.
The roundings to bfloat16 on the way count: a program that leaves them out, or rounds other values in their place, can miss the bound.
Values may be sent and summed in bfloat16 or wider, within the bound.
A program may use at most 64 MiB of HBM per device.

v0:
```python
import jax
import jax.numpy as jnp
from jax import lax
from jax.sharding import PartitionSpec as P

SECOND_DILATION = 4096


def passed_along(array, axis, by):
    length = lax.axis_size(axis)
    pairs = [(i, i + by) for i in range(length) if 0 <= i + by < length]
    return lax.ppermute(array, axis, pairs)


def gated_units(current, earlier, weights, biases):
    row_total = current.shape[0]
    groups = weights.shape[0]
    group_width = weights.shape[1] // 2
    stacked = jnp.concatenate(
        [
            earlier.reshape(row_total, groups, group_width),
            current.reshape(row_total, groups, group_width),
        ],
        axis=2,
    )
    mixed = (
        jnp.einsum("rgk,gkn->rgn", stacked, weights, preferred_element_type=jnp.float32)
        + biases[None, :, :]
    )
    hidden = jnp.tanh(mixed[:, :, :group_width]) * jax.nn.sigmoid(mixed[:, :, group_width:])
    return hidden.reshape(row_total, groups * group_width).astype(jnp.bfloat16)


def residual_layer(current, earlier, weights, biases, mix_cols):
    hidden = gated_units(current, earlier, weights, biases)
    mixing = jnp.dot(
        lax.all_gather(hidden, "chan", axis=1, tiled=True),
        mix_cols,
        preferred_element_type=jnp.float32,
    )
    return (current.astype(jnp.float32) + mixing).astype(jnp.bfloat16)


def shards(signal, kernel_weight_stack, conv_bias, mix_weight):
    round_total_count, chan_width = signal.shape
    distant_reach = SECOND_DILATION // round_total_count
    last_round = passed_along(signal[round_total_count - 1 :], "tm", 1)
    with_edge = jnp.concatenate([last_round, signal], axis=0)
    earlier = with_edge[:-1]
    layer_one = residual_layer(signal, earlier, kernel_weight_stack[0], conv_bias[0], mix_weight[0])
    distant = passed_along(layer_one, "tm", distant_reach)
    output = residual_layer(layer_one, distant, kernel_weight_stack[1], conv_bias[1], mix_weight[1])
    return output


def solution(mesh):
    placed = (
        P(("parts", "tm"), "chan"),
        P(None, "chan", None, None),
        P(None, "chan", None),
        P(None, None, "chan"),
    )
    return jax.shard_map(
        shards, mesh=mesh, in_specs=placed, out_specs=P(("parts", "tm"), "chan"), check_vma=False
    )
```

profile of v0, /device:TPU:27, one launch (start us, length us, event | category | flops | bytes accessed | tf_op | source)
XLA Modules:
  0.0 120.9 jit_solution(179060073413924786)
XLA Ops:
  6.5 0.0 all-gather.3.cloned.1.call-start
  6.5 0.7 slice.36
  7.2 0.2 copy.13
  7.4 1.3 %collective-permute-start = (bf16[1,512]{0,1:T(8,128)(2,1)S(1)}, bf16[1,512]{0,1:T(8,128)(2,1)S(1)}, u32[]{:S(2)}, u32[]{:S(2)}) collective-permute-start(bf16[1,512]{0,1:T(8,128)(2,1)S(1)} %copy.13), channel_id=1, source_target_pairs={{0,2},{2,4},{4,6},{6,8},{8,10},{10,12},{12,14},{1,3},{3,5},{5,7},{... | collective-permute-start | bytes 3080 | tf_op jit(solution)/shard_map/ppermute | solution.py:12
  8.7 0.7 slice_bitcast_fusion
  9.4 1.5 %copy.12 = bf16[1024,512]{0,1:T(8,128)(2,1)S(1)} copy(bf16[1024,512]{1,0:T(8,128)(2,1)} %param.4) | data formatting | bytes 2097152 | tf_op args[0]
  10.9 1.1 copy.17
  12.0 1.7 %collective-permute-done = bf16[1,512]{0,1:T(8,128)(2,1)S(1)} collective-permute-done((bf16[1,512]{0,1:T(8,128)(2,1)S(1)}, bf16[1,512]{0,1:T(8,128)(2,1)S(1)}, u32[]{:S(2)}, u32[]{:S(2)}) %collective-permute-start) | collective-permute-done | bytes 1056 | tf_op jit(solution)/shard_map/ppermute | solution.py:12
  13.7 1.5 %pad_maximum_fusion = bf16[1024,512]{0,1:T(8,128)(2,1)} fusion(bf16[1024,512]{0,1:T(8,128)(2,1)S(1)} %copy.12, bf16[1,512]{0,1:T(8,128)(2,1)S(1)} %collective-permute-done), kind=kLoop, calls=%fused_computation.24 | loop fusion | flops 2097152 | bytes 2098176 | tf_op jit(solution)/shard_map/concatenate | solution.py:48
  15.2 2.8 %copy.16 = bf16[1024,8,64]{2,0,1:T(8,128)(2,1)} copy(bf16[1024,8,64]{0,2,1:T(8,128)(2,1)} %bitcast.33) | data formatting | bytes 2097152 | tf_op jit(solution)/shard_map/reshape | solution.py:21
  18.0 3.1 %add_bitcast_fusion.1 = f32[1024,8,128]{0,2,1:T(8,128)S(1)} fusion(bf16[1024,8,64]{2,0,1:T(8,128)(2,1)S(1)} %copy.17, bf16[1024,8,64]{2,0,1:T(8,128)(2,1)} %copy.16, f32[8,128]{1,0:T(8,128)S(1)} %get-tuple-element.6, bf16[2,8,128,128]{3,2,1,0:T(8,128)(2,1)} %param.5), kind=kOutput, calls=%fused_computation.1 | convolution fusion | flops 273678336 | bytes 7606272 | tf_op jit(solution)/shard_map/rgk,gkn->rgn/dot_general | solution.py:27
  21.1 1.8 %fusion.14 = bf16[1024,8,64]{0,2,1:T(8,128)(2,1)} fusion(f32[1024,8,128]{0,2,1:T(8,128)S(1)} %add_bitcast_fusion.1), kind=kLoop, calls=%fused_computation.22 | loop fusion | flops 2621440 | bytes 5242880 | tf_op jit(solution)/shard_map/convert_element_type | solution.py:31
  22.8 0.0 all-gather.3.cloned.1.call-update
  22.9 0.0 all-gather.5.cloned.1.call-start
  22.9 13.2 %all-gather.3.cloned.1.call-done = bf16[1024,1024]{0,1:T(8,128)(2,1)} async-done(((bf16[1024,512]{0,1:T(8,128)(2,1)}), bf16[1024,1024]{0,1:T(8,128)(2,1)}) %all-gather.3.cloned.1.call-update) | async-done | bytes 2097168 | tf_op jit(solution)/shard_map/all_gather | solution.py:37
  36.2 3.1 %add_convert_fusion.1 = bf16[1024,512]{0,1:T(8,128)(2,1)S(1)} fusion(bf16[1024,512]{0,1:T(8,128)(2,1)S(1)} %copy.12, bf16[1024,1024]{0,1:T(8,128)(2,1)} %all-gather.3.cloned.1.call-done, bf16[2,1024,512]{2,1,0:T(8,128)(2,1)} %param.7), kind=kOutput, calls=%fused_computation.21 | convolution fusion | flops 1075314688 | bytes 5242880 | tf_op jit(solution)/shard_map/dot_general | solution.py:36
  39.3 1.3 %collective-permute-start.1 = (bf16[1024,512]{0,1:T(8,128)(2,1)S(1)}, bf16[1024,512]{0,1:T(8,128)(2,1)}, u32[]{:S(2)}, u32[]{:S(2)}) collective-permute-start(bf16[1024,512]{0,1:T(8,128)(2,1)S(1)} %add_convert_fusion.1), channel_id=1, source_target_pairs={{0,8},{2,10},{4,12},{6,14},{1,9},{3,11},{5,13},{7,15},{16,24},{18,... | collective-permute-start | bytes 3145736 | tf_op jit(solution)/shard_map/ppermute | solution.py:12
  40.6 1.1 copy.20
  41.7 48.1 %collective-permute-done.1 = bf16[1024,512]{0,1:T(8,128)(2,1)} collective-permute-done((bf16[1024,512]{0,1:T(8,128)(2,1)S(1)}, bf16[1024,512]{0,1:T(8,128)(2,1)}, u32[]{:S(2)}, u32[]{:S(2)}) %collective-permute-start.1) | collective-permute-done | bytes 1048608 | tf_op jit(solution)/shard_map/ppermute | solution.py:12
  89.8 2.8 %copy.19 = bf16[1024,8,64]{2,0,1:T(8,128)(2,1)} copy(bf16[1024,8,64]{0,2,1:T(8,128)(2,1)} %bitcast.7) | data formatting | bytes 2097152 | tf_op jit(solution)/shard_map/reshape | solution.py:21
  92.5 3.1 %add_bitcast_fusion = f32[1024,8,128]{0,2,1:T(8,128)S(1)} fusion(bf16[1024,8,64]{2,0,1:T(8,128)(2,1)S(1)} %copy.20, bf16[1024,8,64]{2,0,1:T(8,128)(2,1)} %copy.19, f32[8,128]{1,0:T(8,128)S(1)} %get-tuple-element.5, bf16[2,8,128,128]{3,2,1,0:T(8,128)(2,1)} %param.5), kind=kOutput, calls=%fused_computation | convolution fusion | flops 273678336 | bytes 7606272 | tf_op jit(solution)/shard_map/rgk,gkn->rgn/dot_general | solution.py:27
  95.6 1.8 %fusion.15 = bf16[1024,8,64]{0,2,1:T(8,128)(2,1)} fusion(f32[1024,8,128]{0,2,1:T(8,128)S(1)} %add_bitcast_fusion), kind=kLoop, calls=%fused_computation.23 | loop fusion | flops 2621440 | bytes 5242880 | tf_op jit(solution)/shard_map/convert_element_type | solution.py:31
  97.4 0.0 all-gather.5.cloned.1.call-update
  97.4 12.2 %all-gather.5.cloned.1.call-done = bf16[1024,1024]{0,1:T(8,128)(2,1)} async-done(((bf16[1024,512]{0,1:T(8,128)(2,1)}), bf16[1024,1024]{0,1:T(8,128)(2,1)}) %all-gather.5.cloned.1.call-update) | async-done | bytes 2097168 | tf_op jit(solution)/shard_map/all_gather | solution.py:37
  109.6 3.1 %add_convert_fusion = bf16[1024,512]{0,1:T(8,128)(2,1)S(1)} fusion(bf16[1024,512]{0,1:T(8,128)(2,1)S(1)} %add_convert_fusion.1, bf16[1024,1024]{0,1:T(8,128)(2,1)} %all-gather.5.cloned.1.call-done, bf16[2,1024,512]{2,1,0:T(8,128)(2,1)} %param.7), kind=kOutput, calls=%fused_computation.20 | convolution fusion | flops 1075314688 | bytes 5242880 | tf_op jit(solution)/shard_map/dot_general | solution.py:36
  112.7 1.3 %copy.23 = bf16[1024,512]{1,0:T(8,128)(2,1)} copy(bf16[1024,512]{0,1:T(8,128)(2,1)S(1)} %add_convert_fusion) | data formatting | bytes 2097152 | tf_op jit(solution)/shard_map/convert_element_type | solution.py:41
Async XLA Ops:
  6.5 29.6 %all-gather.3.cloned.1.call-start = ((), (), s32[]{:S(2)}) async-start(), calls=%async_computation | async-start | bytes 3145728 | tf_op jit(solution)/shard_map/all_gather | solution.py:37
  7.4 6.3 %collective-permute-start = (bf16[1,512]{0,1:T(8,128)(2,1)S(1)}, bf16[1,512]{0,1:T(8,128)(2,1)S(1)}, u32[]{:S(2)}, u32[]{:S(2)}) collective-permute-start(bf16[1,512]{0,1:T(8,128)(2,1)S(1)} %copy.13), channel_id=1, source_target_pairs={{0,2},{2,4},{4,6},{6,8},{8,10},{10,12},{12,14},{1,3},{3,5},{5,7},{... | collective-permute-start | bytes 3080 | tf_op jit(solution)/shard_map/ppermute | solution.py:12
  22.9 86.7 %all-gather.5.cloned.1.call-start = ((), (), s32[]{:S(2)}) async-start(), calls=%async_computation.1 | async-start | bytes 3145728 | tf_op jit(solution)/shard_map/all_gather | solution.py:37
  39.3 50.5 %collective-permute-start.1 = (bf16[1024,512]{0,1:T(8,128)(2,1)S(1)}, bf16[1024,512]{0,1:T(8,128)(2,1)}, u32[]{:S(2)}, u32[]{:S(2)}) collective-permute-start(bf16[1024,512]{0,1:T(8,128)(2,1)S(1)} %add_convert_fusion.1), channel_id=1, source_target_pairs={{0,8},{2,10},{4,12},{6,14},{1,9},{3,11},{5,13},{7,15},{16,24},{18,... | collective-permute-start | bytes 3145736 | tf_op jit(solution)/shard_map/ppermute | solution.py:12
Sparse Core Ops, SparseCore 0:
  23.0 13.1 all-gather.2
  97.5 11.9 all-gather.4
where the time goes:
time: 122 us; the launch traced here: 121 us
  waiting for transfers between devices  75.2 us (62%)
  between operations  13.5 us (11%)
  matrix products  12.4 us (10%)
  local copies, waits for them, and re-layouts  12.1 us (10%)
  other arithmetic  5.09 us (4%)
  starting transfers between devices  2.63 us (2%)
    ppermute x2, waiting for transfers between devices, passed_along(): return lax.ppermute(array, axis, pairs)  49.8 us
    all_gather x2, waiting for transfers between devices, residual_layer(): lax.all_gather(hidden, 'chan', axis=1, tiled=True)  25.4 us
    dot_general x2, matrix products, residual_layer(): jnp.dot(lax.all_gather(hidden, 'chan', axis=1, tiled=True), mix_cols, pre...  6.28 us
    dot_general x2, matrix products, gated_units(): jnp.einsum('rgk,gkn->rgn', stacked, weights, preferred_element_type=jnp.f...  6.16 us
    reshape x2, local copies, waits for them, and re-layouts, gated_units(): earlier.reshape(row_total, groups, group_width)  5.54 us
    convert_element_type x2, other arithmetic, gated_units(): return hidden.reshape(row_total, groups * group_width).astype(jnp.bfloat16)  3.58 us
    ppermute x2, starting transfers between devices, passed_along(): return lax.ppermute(array, axis, pairs)  2.58 us
  transfers between devices with their start and end apart: 4, of which 4 were waited for; matrix products, arithmetic and copies ran while one was open for 4% of the time, Pallas kernels for 0%

commit v1 on v0

v1 whole, which is shorter than its diff:
```python
import functools

import jax
import jax.numpy as jnp
from jax import lax
from jax.experimental import pallas as pl
from jax.experimental.pallas import tpu as pltpu
from jax.sharding import PartitionSpec as P

SECOND_DILATION = 4096
EDGE = 16
MESH = pl.DeviceIdType.MESH


def layers_kernel(
    length, reach, rows, raw_rows,
    sig, kws, bias, mix, out,
    xbuf, raw, far, x1, hid, oth, kv, wp, bv, bp, mv, obuf,
    load_sem, edge_sem, raw_sem, fwd_sem, x1_send, x1_recv, hid_send, hid_recv, out_sem,
):
    total, width = sig.shape
    groups, taps = kws.shape[1], kws.shape[2]
    half = taps // 2
    pairs = groups // 2
    chunks, raw_chunks = total // rows, raw_rows // rows
    part, t, c = lax.axis_index("parts"), lax.axis_index("tm"), lax.axis_index("chan")
    has_next, has_prev = t < length - 1, t > 0
    sends, receives = t < length - reach, t >= reach

    def at(step):
        return (part, lax.rem(t + step + length, length), c)

    peer = (part, t, 1 - c)

    barrier = pltpu.get_barrier_semaphore()
    for there, step in ((has_next, 1), (has_prev, -1), (sends, reach), (receives, -reach)):

        @pl.when(there)
        def _(step=step):
            pl.semaphore_signal(barrier, inc=1, device_id=at(step), device_id_type=MESH)

    pl.semaphore_signal(barrier, inc=1, device_id=peer, device_id_type=MESH)

    loads = [
        pltpu.make_async_copy(src, dst, load_sem.at[i])
        for i, (src, dst) in enumerate(
            (
                (kws, kv),
                (bias, bv),
                (sig, xbuf.at[pl.ds(EDGE, total)]),
                (mix.at[0], mv.at[0]),
                (mix.at[1], mv.at[1]),
            )
        )
    ]
    for copy in loads:
        copy.start()

    partners = 1
    for there in (has_next, has_prev, sends, receives):
        partners = partners + there.astype(jnp.int32)
    pl.semaphore_wait(barrier, partners)

    def remote(src, dst, send, recv, to):
        return pltpu.make_async_remote_copy(
            src_ref=src, dst_ref=dst, send_sem=send, recv_sem=recv, device_id=to, device_id_type=MESH
        )

    edge_copy = remote(
        sig.at[pl.ds(total - EDGE, EDGE)], xbuf.at[pl.ds(0, EDGE)], edge_sem.at[0], edge_sem.at[1], at(1)
    )
    raw_copy = remote(
        sig.at[pl.ds(0, raw_rows)], raw.at[pl.ds(EDGE, raw_rows)], raw_sem.at[0], raw_sem.at[1], at(reach)
    )
    raw_edge_copy = remote(
        xbuf.at[pl.ds(0, EDGE)], raw.at[pl.ds(0, EDGE)], fwd_sem.at[0], fwd_sem.at[1], at(reach)
    )
    pl.when(has_next)(edge_copy.start)
    pl.when(sends)(raw_copy.start)

    def block(k, offset=0, size=rows):
        return pl.ds(pl.multiple_of(k * rows + offset, EDGE), size)

    def x1_copy(k):
        return remote(x1.at[block(k)], far.at[block(k)], x1_send.at[k], x1_recv.at[k], at(reach))

    def hid_copy(k):
        return remote(hid.at[block(k)], oth.at[block(k)], hid_send.at[k], hid_recv.at[k], peer)

    def out_copy(k):
        return pltpu.make_async_copy(obuf.at[block(k)], out.at[block(k)], out_sem.at[k])

    def pack_weights(layer):
        zero = jnp.zeros((half, half), jnp.bfloat16)
        for p in range(pairs):
            even, odd = kv[layer, 2 * p], kv[layer, 2 * p + 1]
            for tap in range(2):
                e, o = even[tap * half : (tap + 1) * half], odd[tap * half : (tap + 1) * half]
                top, low = tap * taps, tap * taps + half
                wp[layer, p, top : top + half, :] = jnp.concatenate(
                    [e[:, :half], zero, e[:, half:], zero], axis=1
                )
                wp[layer, p, low : low + half, :] = jnp.concatenate(
                    [zero, o[:, :half], zero, o[:, half:]], axis=1
                )
            be, bo = bv[layer, 2 * p : 2 * p + 1], bv[layer, 2 * p + 1 : 2 * p + 2]
            at_row = layer * pairs + p
            bp[at_row : at_row + 1, :] = jnp.concatenate(
                [be[:, :half], bo[:, :half], be[:, half:], bo[:, half:]], axis=1
            )

    def gated(slot, layer, earlier, current):
        for p in range(pairs):
            cols = slice(p * taps, (p + 1) * taps)
            z = jnp.dot(
                jnp.concatenate([earlier[:, cols], current[:, cols]], axis=1),
                wp[layer, p],
                preferred_element_type=jnp.float32,
            )
            row = layer * pairs + p
            z = z + bp[row : row + 1, :]
            h = jnp.tanh(z[:, :taps]) * (0.5 * jnp.tanh(0.5 * z[:, taps:]) + 0.5)
            hid[block(slot), cols] = h.astype(jnp.bfloat16)
        hid_copy(slot).start()

    def mixed(slot, layer, current):
        mine = mv[layer, pl.ds(pl.multiple_of(c * width, width), width), :]
        theirs = mv[layer, pl.ds(pl.multiple_of((1 - c) * width, width), width), :]
        acc = jnp.dot(hid[block(slot)], mine, preferred_element_type=jnp.float32)
        hid_copy(slot).wait_recv()
        acc = acc + jnp.dot(oth[block(slot)], theirs, preferred_element_type=jnp.float32)
        return (current.astype(jnp.float32) + acc).astype(jnp.bfloat16)

    def first_gated(buf, k, slot):
        window = buf[block(k, size=rows + EDGE)]
        shifted = pltpu.roll(window.astype(jnp.float32), 1, 0)[EDGE:].astype(jnp.bfloat16)
        gated(slot, 0, shifted, window[EDGE:])

    def own_finish(k):
        x1[block(k)] = mixed(k, 0, xbuf[block(k, EDGE)])

        @pl.when(jnp.logical_and(sends, k >= raw_chunks))
        def _():
            x1_copy(k).start()

    loads[0].wait()
    loads[1].wait()
    pack_weights(0)

    @pl.when(jnp.logical_not(has_prev))
    def _():
        xbuf[:EDGE] = jnp.zeros((EDGE, width), jnp.bfloat16)

    @pl.when(jnp.logical_not(receives))
    def _():
        far[...] = jnp.zeros((total, width), jnp.bfloat16)

    pl.when(has_prev)(edge_copy.wait_recv)
    pl.when(sends)(raw_edge_copy.start)
    loads[2].wait()
    first_gated(xbuf, 0, 0)
    loads[3].wait()

    @pl.loop(1, chunks)
    def _(k):
        first_gated(xbuf, k, k)
        own_finish(k - 1)

    own_finish(chunks - 1)

    pack_weights(1)
    loads[4].wait()

    @pl.when(receives)
    def _():
        raw_copy.wait_recv()
        raw_edge_copy.wait_recv()

        @pl.loop(0, raw_chunks)
        def _(k):
            first_gated(raw, k, chunks + k)
            far[block(k)] = mixed(chunks + k, 0, raw[block(k, EDGE)])

    @pl.loop(0, chunks)
    def _(k):
        @pl.when(jnp.logical_and(receives, k >= raw_chunks))
        def _():
            x1_copy(k).wait_recv()

        slot = chunks + raw_chunks + k
        current = x1[block(k)]
        gated(slot, 1, far[block(k)], current)
        obuf[block(k)] = mixed(slot, 1, current)
        out_copy(k).start()

    @pl.loop(0, chunks)
    def _(k):
        out_copy(k).wait()
        hid_copy(k).wait_send()
        hid_copy(chunks + raw_chunks + k).wait_send()

        @pl.when(jnp.logical_and(sends, k >= raw_chunks))
        def _():
            x1_copy(k).wait_send()

    @pl.when(receives)
    def _():
        @pl.loop(0, raw_chunks)
        def _(k):
            hid_copy(chunks + k).wait_send()

    pl.when(has_next)(edge_copy.wait_send)

    @pl.when(sends)
    def _():
        raw_copy.wait_send()
        raw_edge_copy.wait_send()


def shards(length, signal, kernel_weight_stack, conv_bias, mix_weight):
    total, width = signal.shape
    layers, groups, taps, _ = kernel_weight_stack.shape
    reach = SECOND_DILATION // total
    rows, raw_rows = 64, 128
    chunks = total // rows
    slots = 2 * chunks + raw_rows // rows
    bf16, f32 = jnp.bfloat16, jnp.float32
    dma = pltpu.SemaphoreType.DMA
    return pl.pallas_call(
        functools.partial(layers_kernel, length, reach, rows, raw_rows),
        out_shape=jax.ShapeDtypeStruct(signal.shape, bf16),
        in_specs=[pl.BlockSpec(memory_space=pltpu.HBM)] * 4,
        out_specs=pl.BlockSpec(memory_space=pl.ANY),
        scratch_shapes=[
            pltpu.VMEM((EDGE + total, width), bf16),
            pltpu.VMEM((EDGE + raw_rows, width), bf16),
            pltpu.VMEM((total, width), bf16),
            pltpu.VMEM((total, width), bf16),
            pltpu.VMEM((slots * rows, width), bf16),
            pltpu.VMEM((slots * rows, width), bf16),
            pltpu.VMEM(kernel_weight_stack.shape, bf16),
            pltpu.VMEM((layers, groups // 2, 2 * taps, 2 * taps), bf16),
            pltpu.VMEM(conv_bias.shape, f32),
            pltpu.VMEM((layers * groups // 2, 2 * taps), f32),
            pltpu.VMEM(mix_weight.shape, bf16),
            pltpu.VMEM((total, width), bf16),
            dma((5,)),
            dma((2,)),
            dma((2,)),
            dma((2,)),
            dma((chunks,)),
            dma((chunks,)),
            dma((slots,)),
            dma((slots,)),
            dma((chunks,)),
        ],
        compiler_params=pltpu.CompilerParams(
            collective_id=0, has_side_effects=True, vmem_limit_bytes=40 << 20
        ),
    )(signal, kernel_weight_stack, conv_bias, mix_weight)


def solution(mesh):
    placed = (
        P(("parts", "tm"), "chan"),
        P(None, "chan", None, None),
        P(None, "chan", None),
        P(None, None, "chan"),
    )
    return jax.shard_map(
        functools.partial(shards, mesh.shape["tm"]),
        mesh=mesh,
        in_specs=placed,
        out_specs=P(("parts", "tm"), "chan"),
        check_vma=False,
    )
```

time: 122 us -> 65.6 us (0.54)
  waiting for transfers between devices: 75.2 us -> 0 us
  Pallas kernels: 0 us -> 59.8 us
  between operations: 13.5 us -> 0.01 us
  matrix products: 12.4 us -> 0 us
  local copies, waits for them, and re-layouts: 12.1 us -> 5.52 us
  other arithmetic: 5.09 us -> 0 us
  starting transfers between devices: 2.63 us -> 0 us
    pallas_call x0 -> x1, Pallas kernels: none -> 59.8 us  [shards(): pl.pallas_call(functools.partial(layers_kernel, length, reach, rows, raw_...]
    ppermute x2 -> x0, waiting for transfers between devices: 49.8 us -> none  [passed_along(): return lax.ppermute(array, axis, pairs)]
    all_gather x2 -> x0, waiting for transfers between devices: 25.4 us -> none  [residual_layer(): lax.all_gather(hidden, 'chan', axis=1, tiled=True)]
    dot_general x4 -> x0, matrix products: 12.4 us -> none  [the longest x2 6.28 us: residual_layer(): jnp.dot(lax.all_gather(hidden, 'chan', axis=1, tiled=True), mix_cols, pre...]
    reshape x4 -> x0, local copies, waits for them, and re-layouts: 7.68 us -> none  [the longest x2 5.54 us: gated_units(): earlier.reshape(row_total, groups, group_width)]
    unnamed x1 -> x9, local copies, waits for them, and re-layouts: 1.48 us -> 5.52 us
    convert_element_type x2 -> x0, other arithmetic: 3.58 us -> none  [gated_units(): return hidden.reshape(row_total, groups * group_width).astype(jnp.bfloat16)]
    ppermute x2 -> x0, starting transfers between devices: 2.58 us -> none  [passed_along(): return lax.ppermute(array, axis, pairs)]
  transfers between devices with their start and end apart: 4 -> 0, of which waited for: 4 -> 0; matrix products, arithmetic and copies ran while one was open for 4% -> 0% of each run, Pallas kernels for 0% -> 0%
where the time goes in v1:
time: 65.6 us; the launch traced here: 65.3 us
  Pallas kernels  59.8 us (91%)
  local copies, waits for them, and re-layouts  5.52 us (8%)
    pallas_call x1, Pallas kernels, shards(): pl.pallas_call(functools.partial(layers_kernel, length, reach, rows, raw_...  59.8 us
    unnamed x9, local copies, waits for them, and re-layouts  5.52 us

profile of v1, /device:TPU:27, one launch (start us, length us, event | category | flops | bytes accessed | tf_op | source)
XLA Modules:
  0.0 65.3 jit_solution(2275709971723892533)
XLA Ops:
  0.0 0.0 copy-start
  0.0 1.6 %copy-done = bf16[2,1024,512]{2,1,0:T(8,128)(2,1)S(1)} copy-done((bf16[2,1024,512]{2,1,0:T(8,128)(2,1)S(1)}, bf16[2,1024,512]{2,1,0:T(8,128)(2,1)}, u32[]{:S(2)}) %copy-start) | copy-done | bytes 2097176
  1.6 0.0 copy-start.1
  1.6 1.2 %copy-done.1 = bf16[1024,512]{1,0:T(8,128)(2,1)S(1)} copy-done((bf16[1024,512]{1,0:T(8,128)(2,1)S(1)}, bf16[1024,512]{1,0:T(8,128)(2,1)}, u32[]{:S(2)}) %copy-start.1) | copy-done | bytes 1048600
  2.8 0.0 copy-start.2
  2.8 1.0 %copy-done.2 = bf16[2,8,128,128]{3,2,1,0:T(8,128)(2,1)S(1)} copy-done((bf16[2,8,128,128]{3,2,1,0:T(8,128)(2,1)S(1)}, bf16[2,8,128,128]{3,2,1,0:T(8,128)(2,1)}, u32[]{:S(2)}) %copy-start.2) | copy-done | bytes 524312
  3.9 0.0 copy-start.3
  3.9 0.7 %copy-done.3 = f32[2,8,128]{2,1,0:T(8,128)S(1)} copy-done((f32[2,8,128]{2,1,0:T(8,128)S(1)}, f32[2,8,128]{2,1,0:T(8,128)}, u32[]{:S(2)}) %copy-start.3) | copy-done | bytes 8216
  4.6 59.8 %shard_map.46 = bf16[1024,512]{1,0:T(8,128)(2,1)S(1)} custom-call(bf16[1024,512]{1,0:T(8,128)(2,1)S(1)} %copy-done.1, bf16[2,8,128,128]{3,2,1,0:T(8,128)(2,1)S(1)} %copy-done.2, f32[2,8,128]{2,1,0:T(8,128)S(1)} %copy-done.3, bf16[2,1024,512]{2,1,0:T(8,128)(2,1)S(1)} %copy-done), custom_call_target="tpu_custom_call" | custom-call | tf_op jit(solution)/shard_map/pallas_call | solution.py:229
  64.4 1.0 %copy.6 = bf16[1024,512]{1,0:T(8,128)(2,1)} copy(bf16[1024,512]{1,0:T(8,128)(2,1)S(1)} %shard_map.46) | data formatting | bytes 2097152
Async XLA Ops:
  0.0 1.6 %copy-start = (bf16[2,1024,512]{2,1,0:T(8,128)(2,1)S(1)}, bf16[2,1024,512]{2,1,0:T(8,128)(2,1)}, u32[]{:S(2)}) copy-start(bf16[2,1024,512]{2,1,0:T(8,128)(2,1)} %mix.1) | copy-start | bytes 6291460
  1.6 1.2 %copy-start.1 = (bf16[1024,512]{1,0:T(8,128)(2,1)S(1)}, bf16[1024,512]{1,0:T(8,128)(2,1)}, u32[]{:S(2)}) copy-start(bf16[1024,512]{1,0:T(8,128)(2,1)} %sig.1) | copy-start | bytes 3145732
  2.8 1.0 %copy-start.2 = (bf16[2,8,128,128]{3,2,1,0:T(8,128)(2,1)S(1)}, bf16[2,8,128,128]{3,2,1,0:T(8,128)(2,1)}, u32[]{:S(2)}) copy-start(bf16[2,8,128,128]{3,2,1,0:T(8,128)(2,1)} %kws.1) | copy-start | bytes 1572868
  3.9 0.7 %copy-start.3 = (f32[2,8,128]{2,1,0:T(8,128)S(1)}, f32[2,8,128]{2,1,0:T(8,128)}, u32[]{:S(2)}) copy-start(f32[2,8,128]{2,1,0:T(8,128)} %bias.1) | copy-start | bytes 24580

commit v2 on v1

--- a/solution.py
+++ b/solution.py
@@ -221,7 +221,7 @@
     total, width = signal.shape
     layers, groups, taps, _ = kernel_weight_stack.shape
     reach = SECOND_DILATION // total
-    rows, raw_rows = 64, 128
+    rows, raw_rows = 128, 128
     chunks = total // rows
     slots = 2 * chunks + raw_rows // rows
     bf16, f32 = jnp.bfloat16, jnp.float32

time: 65.6 us -> 58.1 us (0.89)
  Pallas kernels: 59.8 us -> 52.3 us
    pallas_call x1, Pallas kernels: 59.8 us -> 52.3 us  [shards(): pl.pallas_call(functools.partial(layers_kernel, length, reach, rows, raw_...]
where the time goes in v2:
time: 58.1 us; the launch traced here: 57.8 us
  Pallas kernels  52.3 us (90%)
  local copies, waits for them, and re-layouts  5.52 us (10%)
    pallas_call x1, Pallas kernels, shards(): pl.pallas_call(functools.partial(layers_kernel, length, reach, rows, raw_...  52.3 us
    unnamed x9, local copies, waits for them, and re-layouts  5.52 us

profile of v2, /device:TPU:27, one launch (start us, length us, event | category | flops | bytes accessed | tf_op | source)
XLA Modules:
  0.0 57.8 jit_solution(7697225833301454486)
XLA Ops:
  0.0 0.0 copy-start
  0.0 1.6 %copy-done = bf16[2,1024,512]{2,1,0:T(8,128)(2,1)S(1)} copy-done((bf16[2,1024,512]{2,1,0:T(8,128)(2,1)S(1)}, bf16[2,1024,512]{2,1,0:T(8,128)(2,1)}, u32[]{:S(2)}) %copy-start) | copy-done | bytes 2097176
  1.6 0.0 copy-start.1
  1.6 1.2 %copy-done.1 = bf16[1024,512]{1,0:T(8,128)(2,1)S(1)} copy-done((bf16[1024,512]{1,0:T(8,128)(2,1)S(1)}, bf16[1024,512]{1,0:T(8,128)(2,1)}, u32[]{:S(2)}) %copy-start.1) | copy-done | bytes 1048600
  2.8 0.0 copy-start.2
  2.8 1.0 %copy-done.2 = bf16[2,8,128,128]{3,2,1,0:T(8,128)(2,1)S(1)} copy-done((bf16[2,8,128,128]{3,2,1,0:T(8,128)(2,1)S(1)}, bf16[2,8,128,128]{3,2,1,0:T(8,128)(2,1)}, u32[]{:S(2)}) %copy-start.2) | copy-done | bytes 524312
  3.9 0.0 copy-start.3
  3.9 0.7 %copy-done.3 = f32[2,8,128]{2,1,0:T(8,128)S(1)} copy-done((f32[2,8,128]{2,1,0:T(8,128)S(1)}, f32[2,8,128]{2,1,0:T(8,128)}, u32[]{:S(2)}) %copy-start.3) | copy-done | bytes 8216
  4.6 52.3 %shard_map.46 = bf16[1024,512]{1,0:T(8,128)(2,1)S(1)} custom-call(bf16[1024,512]{1,0:T(8,128)(2,1)S(1)} %copy-done.1, bf16[2,8,128,128]{3,2,1,0:T(8,128)(2,1)S(1)} %copy-done.2, f32[2,8,128]{2,1,0:T(8,128)S(1)} %copy-done.3, bf16[2,1024,512]{2,1,0:T(8,128)(2,1)S(1)} %copy-done), custom_call_target="tpu_custom_call" | custom-call | tf_op jit(solution)/shard_map/pallas_call | solution.py:229
  56.8 1.0 %copy.6 = bf16[1024,512]{1,0:T(8,128)(2,1)} copy(bf16[1024,512]{1,0:T(8,128)(2,1)S(1)} %shard_map.46) | data formatting | bytes 2097152
Async XLA Ops:
  0.0 1.6 %copy-start = (bf16[2,1024,512]{2,1,0:T(8,128)(2,1)S(1)}, bf16[2,1024,512]{2,1,0:T(8,128)(2,1)}, u32[]{:S(2)}) copy-start(bf16[2,1024,512]{2,1,0:T(8,128)(2,1)} %mix.1) | copy-start | bytes 6291460
  1.6 1.2 %copy-start.1 = (bf16[1024,512]{1,0:T(8,128)(2,1)S(1)}, bf16[1024,512]{1,0:T(8,128)(2,1)}, u32[]{:S(2)}) copy-start(bf16[1024,512]{1,0:T(8,128)(2,1)} %sig.1) | copy-start | bytes 3145732
  2.8 1.0 %copy-start.2 = (bf16[2,8,128,128]{3,2,1,0:T(8,128)(2,1)S(1)}, bf16[2,8,128,128]{3,2,1,0:T(8,128)(2,1)}, u32[]{:S(2)}) copy-start(bf16[2,8,128,128]{3,2,1,0:T(8,128)(2,1)} %kws.1) | copy-start | bytes 1572868
  3.9 0.7 %copy-start.3 = (f32[2,8,128]{2,1,0:T(8,128)S(1)}, f32[2,8,128]{2,1,0:T(8,128)}, u32[]{:S(2)}) copy-start(f32[2,8,128]{2,1,0:T(8,128)} %bias.1) | copy-start | bytes 24580

commit v3 on v2

--- a/solution.py
+++ b/solution.py
@@ -47,14 +47,18 @@
             (
                 (kws, kv),
                 (bias, bv),
-                (sig, xbuf.at[pl.ds(EDGE, total)]),
+                (sig.at[pl.ds(raw_rows, total - raw_rows)], xbuf.at[pl.ds(EDGE + raw_rows, total - raw_rows)]),
                 (mix.at[0], mv.at[0]),
                 (mix.at[1], mv.at[1]),
             )
         )
     ]
-    for copy in loads:
-        copy.start()
+    head_copy = pltpu.make_async_copy(
+        sig.at[pl.ds(0, raw_rows)], xbuf.at[pl.ds(EDGE, raw_rows)], load_sem.at[5]
+    )
+    head_copy.start()
+    for i in (2, 0, 1, 3, 4):
+        loads[i].start()
 
     partners = 1
     for there in (has_next, has_prev, sends, receives):
@@ -67,16 +71,18 @@
         )
 
     edge_copy = remote(
-        sig.at[pl.ds(total - EDGE, EDGE)], xbuf.at[pl.ds(0, EDGE)], edge_sem.at[0], edge_sem.at[1], at(1)
+        xbuf.at[pl.ds(total, EDGE)], xbuf.at[pl.ds(0, EDGE)], edge_sem.at[0], edge_sem.at[1], at(1)
     )
     raw_copy = remote(
-        sig.at[pl.ds(0, raw_rows)], raw.at[pl.ds(EDGE, raw_rows)], raw_sem.at[0], raw_sem.at[1], at(reach)
+        xbuf.at[pl.ds(EDGE, raw_rows)], raw.at[pl.ds(EDGE, raw_rows)], raw_sem.at[0], raw_sem.at[1], at(reach)
     )
     raw_edge_copy = remote(
         xbuf.at[pl.ds(0, EDGE)], raw.at[pl.ds(0, EDGE)], fwd_sem.at[0], fwd_sem.at[1], at(reach)
     )
+    head_copy.wait()
+    pl.when(sends)(raw_copy.start)
+    loads[2].wait()
     pl.when(has_next)(edge_copy.start)
-    pl.when(sends)(raw_copy.start)
 
     def block(k, offset=0, size=rows):
         return pl.ds(pl.multiple_of(k * rows + offset, EDGE), size)
@@ -157,7 +163,6 @@
 
     pl.when(has_prev)(edge_copy.wait_recv)
     pl.when(sends)(raw_edge_copy.start)
-    loads[2].wait()
     first_gated(xbuf, 0, 0)
     loads[3].wait()
 
@@ -244,7 +249,7 @@
             pltpu.VMEM((layers * groups // 2, 2 * taps), f32),
             pltpu.VMEM(mix_weight.shape, bf16),
             pltpu.VMEM((total, width), bf16),
-            dma((5,)),
+            dma((6,)),
             dma((2,)),
             dma((2,)),
             dma((2,)),
@@ -257,7 +262,7 @@
         compiler_params=pltpu.CompilerParams(
             collective_id=0, has_side_effects=True, vmem_limit_bytes=40 << 20
         ),
-    )(signal, kernel_weight_stack, conv_bias, mix_weight)
+    )(*(pltpu.with_memory_space_constraint(a, pltpu.HBM) for a in (signal, kernel_weight_stack, conv_bias, mix_weight)))
 
 
 def solution(mesh):

time: 58.1 us -> 56.3 us (0.969)
  the two profiles are of different devices: /device:TPU:27 before, /device:TPU:17 now
where the time goes in v3:
time: 56.3 us; the launch traced here: 56.2 us
  Pallas kernels  55.2 us (98%)
  local copies, waits for them, and re-layouts  0.97 us (2%)
    pallas_call x1, Pallas kernels, shards(): pl.pallas_call(functools.partial(layers_kernel, length, reach, rows, raw_...  55.2 us

profile of v3, /device:TPU:17, one launch (start us, length us, event | category | flops | bytes accessed | tf_op | source)
XLA Modules:
  0.0 56.2 jit_solution(6162072780438193620)
XLA Ops:
  0.0 55.2 %shard_map.46 = bf16[1024,512]{1,0:T(8,128)(2,1)S(1)} custom-call(bf16[1024,512]{1,0:T(8,128)(2,1)} %sig.1, bf16[2,8,128,128]{3,2,1,0:T(8,128)(2,1)} %kws.1, f32[2,8,128]{2,1,0:T(8,128)} %bias.1, bf16[2,1024,512]{2,1,0:T(8,128)(2,1)} %mix.1), custom_call_target="tpu_custom_call" | custom-call | tf_op jit(solution)/shard_map/pallas_call | solution.py:234
  55.2 1.0 %copy.6 = bf16[1024,512]{1,0:T(8,128)(2,1)} copy(bf16[1024,512]{1,0:T(8,128)(2,1)S(1)} %shard_map.46) | data formatting | bytes 2097152

commit v4 on v3

--- a/solution.py
+++ b/solution.py
@@ -15,7 +15,7 @@
 def layers_kernel(
     length, reach, rows, raw_rows,
     sig, kws, bias, mix, out,
-    xbuf, raw, far, x1, hid, oth, kv, wp, bv, bp, mv, obuf,
+    xbuf, raw, far, x1, hid, oth, kv, wp, bv, bp, mv, obuf, tail,
     load_sem, edge_sem, raw_sem, fwd_sem, x1_send, x1_recv, hid_send, hid_recv, out_sem,
 ):
     total, width = sig.shape
@@ -56,6 +56,8 @@
     head_copy = pltpu.make_async_copy(
         sig.at[pl.ds(0, raw_rows)], xbuf.at[pl.ds(EDGE, raw_rows)], load_sem.at[5]
     )
+    tail_copy = pltpu.make_async_copy(sig.at[pl.ds(total - EDGE, EDGE)], tail, load_sem.at[6])
+    tail_copy.start()
     head_copy.start()
     for i in (2, 0, 1, 3, 4):
         loads[i].start()
@@ -71,7 +73,7 @@
         )
 
     edge_copy = remote(
-        xbuf.at[pl.ds(total, EDGE)], xbuf.at[pl.ds(0, EDGE)], edge_sem.at[0], edge_sem.at[1], at(1)
+        tail, xbuf.at[pl.ds(0, EDGE)], edge_sem.at[0], edge_sem.at[1], at(1)
     )
     raw_copy = remote(
         xbuf.at[pl.ds(EDGE, raw_rows)], raw.at[pl.ds(EDGE, raw_rows)], raw_sem.at[0], raw_sem.at[1], at(reach)
@@ -79,10 +81,10 @@
     raw_edge_copy = remote(
         xbuf.at[pl.ds(0, EDGE)], raw.at[pl.ds(0, EDGE)], fwd_sem.at[0], fwd_sem.at[1], at(reach)
     )
+    tail_copy.wait()
+    pl.when(has_next)(edge_copy.start)
     head_copy.wait()
     pl.when(sends)(raw_copy.start)
-    loads[2].wait()
-    pl.when(has_next)(edge_copy.start)
 
     def block(k, offset=0, size=rows):
         return pl.ds(pl.multiple_of(k * rows + offset, EDGE), size)
@@ -163,6 +165,7 @@
 
     pl.when(has_prev)(edge_copy.wait_recv)
     pl.when(sends)(raw_edge_copy.start)
+    loads[2].wait()
     first_gated(xbuf, 0, 0)
     loads[3].wait()
 
@@ -249,7 +252,8 @@
             pltpu.VMEM((layers * groups // 2, 2 * taps), f32),
             pltpu.VMEM(mix_weight.shape, bf16),
             pltpu.VMEM((total, width), bf16),
-            dma((6,)),
+            pltpu.VMEM((EDGE, width), bf16),
+            dma((7,)),
             dma((2,)),
             dma((2,)),
             dma((2,)),

time: 56.3 us -> 53.4 us (0.948)
  the two profiles are of different devices: /device:TPU:17 before, /device:TPU:27 now
where the time goes in v4:
time: 53.4 us; the launch traced here: 53.3 us
  Pallas kernels  52.3 us (98%)
  local copies, waits for them, and re-layouts  0.97 us (2%)
    pallas_call x1, Pallas kernels, shards(): pl.pallas_call(functools.partial(layers_kernel, length, reach, rows, raw_...  52.3 us

profile of v4, /device:TPU:27, one launch (start us, length us, event | category | flops | bytes accessed | tf_op | source)
XLA Modules:
  0.0 53.3 jit_solution(14985394080132359974)
XLA Ops:
  0.0 52.3 %shard_map.46 = bf16[1024,512]{1,0:T(8,128)(2,1)S(1)} custom-call(bf16[1024,512]{1,0:T(8,128)(2,1)} %sig.1, bf16[2,8,128,128]{3,2,1,0:T(8,128)(2,1)} %kws.1, f32[2,8,128]{2,1,0:T(8,128)} %bias.1, bf16[2,1024,512]{2,1,0:T(8,128)(2,1)} %mix.1), custom_call_target="tpu_custom_call" | custom-call | tf_op jit(solution)/shard_map/pallas_call | solution.py:237
  52.3 1.0 %copy.6 = bf16[1024,512]{1,0:T(8,128)(2,1)} copy(bf16[1024,512]{1,0:T(8,128)(2,1)S(1)} %shard_map.46) | data formatting | bytes 2097152

commit v5 on v4

--- a/solution.py
+++ b/solution.py
@@ -15,7 +15,7 @@
 def layers_kernel(
     length, reach, rows, raw_rows,
     sig, kws, bias, mix, out,
-    xbuf, raw, far, x1, hid, oth, kv, wp, bv, bp, mv, obuf, tail,
+    xbuf, raw, far, x1, hid, oth, kv, wp, bv, bp, mv, obuf, tail, packed, got,
     load_sem, edge_sem, raw_sem, fwd_sem, x1_send, x1_recv, hid_send, hid_recv, out_sem,
 ):
     total, width = sig.shape
@@ -79,7 +79,7 @@
         xbuf.at[pl.ds(EDGE, raw_rows)], raw.at[pl.ds(EDGE, raw_rows)], raw_sem.at[0], raw_sem.at[1], at(reach)
     )
     raw_edge_copy = remote(
-        xbuf.at[pl.ds(0, EDGE)], raw.at[pl.ds(0, EDGE)], fwd_sem.at[0], fwd_sem.at[1], at(reach)
+        packed, got, fwd_sem.at[0], fwd_sem.at[1], at(reach)
     )
     tail_copy.wait()
     pl.when(has_next)(edge_copy.start)
@@ -164,6 +164,12 @@
         far[...] = jnp.zeros((total, width), jnp.bfloat16)
 
     pl.when(has_prev)(edge_copy.wait_recv)
+    last = xbuf[:EDGE].astype(jnp.float32)[EDGE - 1 :]
+    at_row = lax.broadcasted_iota(jnp.int32, (EDGE, 128), 0)
+    tile = jnp.zeros((EDGE, 128), jnp.float32)
+    for j in range(width // 128):
+        tile = jnp.where(at_row == j, last[:, j * 128 : (j + 1) * 128], tile)
+    packed[...] = tile.astype(jnp.bfloat16)
     pl.when(sends)(raw_edge_copy.start)
     loads[2].wait()
     first_gated(xbuf, 0, 0)
@@ -183,6 +189,10 @@
     def _():
         raw_copy.wait_recv()
         raw_edge_copy.wait_recv()
+        tile = got[...].astype(jnp.float32)
+        for j in range(width // 128):
+            row = jnp.broadcast_to(tile[j : j + 1], (EDGE, 128))
+            raw[:EDGE, j * 128 : (j + 1) * 128] = row.astype(jnp.bfloat16)
 
         @pl.loop(0, raw_chunks)
         def _(k):
@@ -253,6 +263,8 @@
             pltpu.VMEM(mix_weight.shape, bf16),
             pltpu.VMEM((total, width), bf16),
             pltpu.VMEM((EDGE, width), bf16),
+            pltpu.VMEM((EDGE, 128), bf16),
+            pltpu.VMEM((EDGE, 128), bf16),
             dma((7,)),
             dma((2,)),
             dma((2,)),

time: 53.4 us -> 52.9 us (level)
  no operation moved by 1% of the time
where the time goes in v5:
time: 52.9 us; the launch traced here: 52.7 us
  Pallas kernels  51.8 us (98%)
  local copies, waits for them, and re-layouts  0.97 us (2%)
    pallas_call x1, Pallas kernels, shards(): pl.pallas_call(functools.partial(layers_kernel, length, reach, rows, raw_...  51.8 us

profile of v5, /device:TPU:27, one launch (start us, length us, event | category | flops | bytes accessed | tf_op | source)
XLA Modules:
  0.0 52.7 jit_solution(5027636849025686480)
XLA Ops:
  0.0 51.8 %shard_map.46 = bf16[1024,512]{1,0:T(8,128)(2,1)S(1)} custom-call(bf16[1024,512]{1,0:T(8,128)(2,1)} %sig.1, bf16[2,8,128,128]{3,2,1,0:T(8,128)(2,1)} %kws.1, f32[2,8,128]{2,1,0:T(8,128)} %bias.1, bf16[2,1024,512]{2,1,0:T(8,128)(2,1)} %mix.1), custom_call_target="tpu_custom_call" | custom-call | tf_op jit(solution)/shard_map/pallas_call | solution.py:247
  51.8 1.0 %copy.6 = bf16[1024,512]{1,0:T(8,128)(2,1)} copy(bf16[1024,512]{1,0:T(8,128)(2,1)S(1)} %shard_map.46) | data formatting | bytes 2097152
